TPU v7x, 32 devices: a whole 2x2x4 slice. The times are simulated.
32 devices in a mesh: grp: 2 (over y), tm: 8 (over z, x), chan: 2 (over core).
Axes of the slice: x: 2, y: 2, z: 4, core: 2. Of those that a mesh axis runs over, the one named last changes fastest.
Arguments:
- signal: bfloat16 [8192, 1024], P(('grp', 'tm'), 'chan'), parts along dimension 0, may hold values from -6 to 6
- filter_weight: bfloat16 [3, 1024, 1024], P(None, 'tm', 'chan'), may hold values from -0.109375 to 0.109375
- gate_weight: bfloat16 [3, 1024, 1024], P(None, 'tm', 'chan'), may hold values from -0.109375 to 0.109375
- filter_bias: float32 [1024], P('chan'), may hold values from -3 to 3
- gate_bias: float32 [1024], P('chan'), may hold values from -3 to 3
- mix_weight: bfloat16 [1024, 1024], P('chan', 'tm'), may hold values from -0.1875 to 0.1875
- cotangent: bfloat16 [8192, 1024], P(('grp', 'tm'), 'chan'), parts along dimension 0, may hold values from -6 to 6
Outputs:
- output: bfloat16 [8192, 1024], P(('grp', 'tm'), 'chan'), parts along dimension 0
- input_grad: bfloat16 [8192, 1024], P(('grp', 'tm'), 'chan'), parts along dimension 0
There are 2 independent parts, one for each index of `grp`. A program takes and returns all parts, laid end to end along the dimension named above; an argument that names none is the same for every part. Nothing has to cross between parts.
All inputs are finite; a program needn't handle non-finite values.
Results may differ from a plain program's by a relative error of at most 0.006.
Values may be sent and summed in bfloat16 or wider, within the bound.
A program may use at most 64 MiB of HBM per device.

v0:
```python
import jax
import jax.numpy as jnp
from jax import lax
from jax.sharding import PartitionSpec as P

KERNEL_TAPS = 3
DILATION_STEPS = 512


def shifted(value, axis, steps):
    count = lax.axis_size(axis)
    leading, last = (max(0, -steps), min(count, count - steps))
    return lax.ppermute(value, axis, [(source, source + steps) for source in range(leading, last)])


def fetch_before(block, receptive_rows):
    sequence_length = block.shape[0]
    hop_count = -(-receptive_rows // sequence_length)
    pieces = []
    for hop_index in range(1, hop_count + 1):
        pieces.insert(0, shifted(block, "tm", hop_index))
    joined = jnp.concatenate(pieces, axis=0)
    return joined


def fetch_after(block, receptive_rows):
    sequence_length = block.shape[0]
    hop_count = -(-receptive_rows // sequence_length)
    pieces = []
    for hop_index in range(1, hop_count + 1):
        pieces.append(shifted(block, "tm", -hop_index))
    joined = jnp.concatenate(pieces, axis=0)
    return joined


def per_device(signal, filter_weight, gate_weight, filter_bias, gate_bias, mix_weight, cotangent):
    sequence_length = signal.shape[0]
    receptive_rows = (KERNEL_TAPS - 1) * DILATION_STEPS
    filter_full, gate_full, mix_full = (
        lax.all_gather(filter_weight, "tm", axis=1, tiled=True),
        lax.all_gather(gate_weight, "tm", axis=1, tiled=True),
        lax.all_gather(mix_weight, "tm", axis=1, tiled=True),
    )
    half_hidden = filter_full.shape[2]
    stacked = jnp.concatenate([filter_full, gate_full], axis=2)
    whole = lax.all_gather(signal, "chan", axis=1, tiled=True)
    earlier = fetch_before(whole, receptive_rows)
    padded_input = jnp.concatenate([earlier, whole], axis=0)
    lagged = jnp.concatenate(
        [
            padded_input[
                receptive_rows
                - tap_position * DILATION_STEPS : receptive_rows
                - tap_position * DILATION_STEPS
                + sequence_length
            ]
            for tap_position in range(KERNEL_TAPS)
        ],
        axis=1,
    )
    bias_both = jnp.concatenate([filter_bias, gate_bias])
    pre_both = (
        jnp.dot(lagged, stacked.reshape(-1, stacked.shape[2]), preferred_element_type=jnp.float32)
        + bias_both
    )
    tangent = jnp.tanh(pre_both[:, :half_hidden])
    opened = jax.nn.sigmoid(pre_both[:, half_hidden:])
    hidden = (tangent * opened).astype(jnp.bfloat16)
    mixed = lax.psum_scatter(
        jnp.dot(hidden, mix_full, preferred_element_type=jnp.float32).astype(jnp.bfloat16),
        "chan",
        scatter_dimension=1,
        tiled=True,
    ).astype(jnp.float32)
    output = (signal.astype(jnp.float32) + mixed).astype(jnp.bfloat16)
    cot_whole = lax.all_gather(cotangent, "chan", axis=1, tiled=True)
    back_hidden = lax.dot_general(
        cot_whole, mix_full, (((1,), (1,)), ((), ())), preferred_element_type=jnp.float32
    )
    grad_filter = (back_hidden * opened * (1.0 - tangent * tangent)).astype(jnp.bfloat16)
    grad_gate = (back_hidden * tangent * opened * (1.0 - opened)).astype(jnp.bfloat16)
    grad_both = jnp.concatenate([grad_filter, grad_gate], axis=1)
    later = fetch_after(grad_both, receptive_rows)
    forward_rows = jnp.concatenate([grad_both, later], axis=0)
    total = jnp.zeros((sequence_length, stacked.shape[1]), jnp.float32)
    for tap_position in range(KERNEL_TAPS):
        input_window = forward_rows[
            tap_position * DILATION_STEPS : tap_position * DILATION_STEPS + sequence_length
        ]
        total = total + lax.dot_general(
            input_window,
            stacked[tap_position],
            (((1,), (1,)), ((), ())),
            preferred_element_type=jnp.float32,
        )
    input_part = lax.psum_scatter(
        total.astype(jnp.bfloat16), "chan", scatter_dimension=1, tiled=True
    ).astype(jnp.float32)
    input_grad = (cotangent.astype(jnp.float32) + input_part).astype(jnp.bfloat16)
    return (output, input_grad)


def solution(mesh):
    in_specs = (
        P(("grp", "tm"), "chan"),
        P(None, "tm", "chan"),
        P(None, "tm", "chan"),
        P("chan"),
        P("chan"),
        P("chan", "tm"),
        P(("grp", "tm"), "chan"),
    )
    out_specs = (P(("grp", "tm"), "chan"), P(("grp", "tm"), "chan"))
    return jax.shard_map(
        per_device, mesh=mesh, in_specs=in_specs, out_specs=out_specs, check_vma=False
    )
```

profile of v0, /device:TPU:18, one launch (start us, length us, event | category | flops | bytes accessed | tf_op | source)
XLA Modules:
  0.0 292.5 jit_solution(15423169669129321825)
XLA Ops:
  7.2 0.0 all-gather.6.cloned.1.call-start
  7.2 0.7 all-gather.6.cloned.1.call-update
  7.9 0.0 all-gather.8.cloned.1.call-start
  7.9 0.7 all-gather.8.cloned.1.call-update
  8.6 0.0 all-gather.10.cloned.1.call-start
  8.7 0.7 all-gather.10.cloned.1.call-update
  9.4 0.0 all-gather.12.cloned.1.call-start
  9.4 0.5 all-gather.12.cloned.1.call-update
  10.0 0.0 all-gather.14.cloned.1.call-start
  10.0 9.9 %all-gather.6.cloned.1.call-done = bf16[512,1024]{1,0:T(8,128)(2,1)} async-done(((bf16[512,512]{1,0:T(8,128)(2,1)}), bf16[512,1024]{1,0:T(8,128)(2,1)}) %all-gather.6.cloned.1.call-update) | async-done | bytes 1048592 | tf_op jit(solution)/shard_map/all_gather | solution.py:46
  19.9 3.4 %collective-permute-start = (bf16[512,1024]{1,0:T(8,128)(2,1)}, bf16[512,1024]{1,0:T(8,128)(2,1)S(1)}, u32[]{:S(2)}, u32[]{:S(2)}) collective-permute-start(bf16[512,1024]{1,0:T(8,128)(2,1)} %all-gather.6.cloned.1.call-done), channel_id=1, source_target_pairs={{0,2},{2,4},{4,6},{6,8},{8,10},{10,12},{12,14},{1,3},{3,5},{5,7},{... | collective-permute-start | bytes 3145736 | tf_op jit(solution)/shard_map/ppermute | solution.py:13
  23.3 1.9 collective-permute-start.1
  25.2 0.0 all-gather.14.cloned.1.call-update
  25.3 0.0 reduce-scatter.3.cloned.1.call-start
  25.3 0.7 pad_maximum_fusion.1
  26.0 81.4 %all-gather.8.cloned.1.call-done = bf16[3,1024,512]{2,1,0:T(8,128)(2,1)} async-done(((bf16[3,128,512]{2,1,0:T(8,128)(2,1)}), bf16[3,1024,512]{2,1,0:T(8,128)(2,1)}) %all-gather.8.cloned.1.call-update) | async-done | bytes 3145744 | tf_op jit(solution)/shard_map/all_gather | solution.py:40
  107.4 3.8 %constant_dynamic-update-slice_fusion.1 = bf16[3,1024,1024]{2,1,0:T(8,128)(2,1)} fusion(bf16[3,1024,512]{2,1,0:T(8,128)(2,1)} %all-gather.8.cloned.1.call-done), kind=kLoop, calls=%fused_computation.27 | loop fusion | bytes 6291456
  111.2 0.0 copy-start.2
  111.3 57.6 %all-gather.10.cloned.1.call-done = bf16[3,1024,512]{2,1,0:T(8,128)(2,1)} async-done(((bf16[3,128,512]{2,1,0:T(8,128)(2,1)}), bf16[3,1024,512]{2,1,0:T(8,128)(2,1)}) %all-gather.10.cloned.1.call-update) | async-done | bytes 3145744 | tf_op jit(solution)/shard_map/all_gather | solution.py:41
  168.8 3.8 %constant_dynamic-update-slice_fusion = bf16[3,1024,1024]{2,1,0:T(8,128)(2,1)} fusion(bf16[3,1024,1024]{2,1,0:T(8,128)(2,1)} %constant_dynamic-update-slice_fusion.1, bf16[3,1024,512]{2,1,0:T(8,128)(2,1)} %all-gather.10.cloned.1.call-done), kind=kLoop, calls=%fused_computation.26 | loop fusion | bytes 6291456 | tf_op jit(solution)/shard_map/concatenate | solution.py:45
  172.7 0.0 collective-permute-done
  172.7 0.0 collective-permute-done.1
  172.7 0.0 copy-done.2
  172.7 7.6 %fusion.9 = f32[512,1024]{1,0:T(8,128)} fusion(bf16[3072,1024]{1,0:T(8,128)(2,1)} %bitcast.18, bf16[512,1024]{1,0:T(8,128)(2,1)S(1)} %collective-permute-done.1, bf16[512,1024]{1,0:T(8,128)(2,1)S(1)} %collective-permute-done, bf16[512,1024]{1,0:T(8,128)(2,1)S(1)} %copy-done.2, f32[1024]{0:T(1024)S(1)} %pad_maximum_fusion.1), kind=kOutput, calls=%fused_computation.13 | convolution fusion | flops 3231186944 | bytes 11538432 | tf_op jit(solution)/shard_map/dot_general | solution.py:63
  180.3 0.0 copy-start.4
  180.3 28.8 %all-gather.12.cloned.1.call-done = bf16[512,1024]{1,0:T(8,128)(2,1)} async-done(((bf16[512,128]{1,0:T(8,128)(2,1)}), bf16[512,1024]{1,0:T(8,128)(2,1)}) %all-gather.12.cloned.1.call-update) | async-done | bytes 1048592 | tf_op jit(solution)/shard_map/all_gather | solution.py:42
  209.1 0.0 copy-start.3
  209.1 3.8 %convolution_convert_fusion = bf16[512,1024]{1,0:T(8,128)(2,1)} fusion(bf16[512,1024]{1,0:T(8,128)(2,1)} %all-gather.12.cloned.1.call-done, f32[512,1024]{1,0:T(8,128)} %fusion.9), kind=kOutput, calls=%fused_computation.14 | convolution fusion | flops 538705920 | bytes 4194304 | tf_op jit(solution)/shard_map/dot_general | solution.py:70
  213.0 0.0 reduce-scatter.3.cloned.1.call-update
  213.0 0.0 reduce-scatter.5.cloned.1.call-start
  213.1 6.8 %all-gather.14.cloned.1.call-done = bf16[512,1024]{1,0:T(8,128)(2,1)} async-done(((bf16[512,512]{1,0:T(8,128)(2,1)}), bf16[512,1024]{1,0:T(8,128)(2,1)}) %all-gather.14.cloned.1.call-update) | async-done | bytes 1048592 | tf_op jit(solution)/shard_map/all_gather | solution.py:76
  219.9 0.0 copy-done.4
  219.9 0.0 copy-done.3
  219.9 2.3 multiply_convert_fusion.1
  222.2 0.0 slice-start
  222.2 0.1 pad_maximum_fusion
  222.4 0.0 slice-start.1
  222.4 2.7 collective-permute-start.2
  225.1 2.5 collective-permute-start.3
  227.6 2.9 fusion.8
  230.5 21.0 %collective-permute-done.2 = bf16[512,1024]{1,0:T(8,128)(2,1)S(1)} collective-permute-done((bf16[512,1024]{1,0:T(8,128)(2,1)S(1)}, bf16[512,1024]{1,0:T(8,128)(2,1)S(1)}, u32[]{:S(2)}, u32[]{:S(2)}) %collective-permute-start.2) | collective-permute-done | bytes 1048608 | tf_op jit(solution)/shard_map/ppermute | solution.py:13
  251.4 0.0 slice-done
  251.4 0.0 slice-done.1
  251.5 1.3 fusion.7
  252.8 0.0 copy-start
  252.8 0.0 copy-start.1
  252.8 0.0 collective-permute-done.3
  252.8 2.3 add_convert_fusion
  255.1 0.0 reduce-scatter.5.cloned.1.call-update
  255.1 0.0 reduce-scatter.3.cloned.1.call-done
  255.2 0.0 copy-done
  255.2 2.0 add_convert_fusion.2
  257.1 26.5 %reduce-scatter.5.cloned.1.call-done = bf16[512,512]{1,0:T(8,128)(2,1)} async-done(((bf16[512,1024]{1,0:T(8,128)(2,1)}), bf16[512,512]{1,0:T(8,128)(2,1)}) %reduce-scatter.5.cloned.1.call-update) | async-done | bytes 524304 | tf_op jit(solution)/shard_map/reduce_scatter | solution.py:96
  283.7 0.0 copy-done.1
  283.7 2.0 add_convert_fusion.1
  (1 shorter events, 0.0 us)
Async XLA Ops:
  7.2 12.8 %all-gather.6.cloned.1.call-start = ((), (), s32[]{:S(2)}) async-start(), calls=%async_computation.2 | async-start | bytes 1572864 | tf_op jit(solution)/shard_map/all_gather | solution.py:46
  7.9 99.5 %all-gather.8.cloned.1.call-start = ((), (), s32[]{:S(2)}) async-start(), calls=%async_computation.3 | async-start | bytes 3538944 | tf_op jit(solution)/shard_map/all_gather | solution.py:40
  8.6 160.2 %all-gather.10.cloned.1.call-start = ((), (), s32[]{:S(2)}) async-start(), calls=%async_computation.4 | async-start | bytes 3538944 | tf_op jit(solution)/shard_map/all_gather | solution.py:41
  9.4 199.8 %all-gather.12.cloned.1.call-start = ((), (), s32[]{:S(2)}) async-start(), calls=%async_computation.5 | async-start | bytes 1179648 | tf_op jit(solution)/shard_map/all_gather | solution.py:42
  10.0 209.9 %all-gather.14.cloned.1.call-start = ((), (), s32[]{:S(2)}) async-start(), calls=%async_computation.7 | async-start | bytes 1572864 | tf_op jit(solution)/shard_map/all_gather | solution.py:76
  19.9 152.8 %collective-permute-start = (bf16[512,1024]{1,0:T(8,128)(2,1)}, bf16[512,1024]{1,0:T(8,128)(2,1)S(1)}, u32[]{:S(2)}, u32[]{:S(2)}) collective-permute-start(bf16[512,1024]{1,0:T(8,128)(2,1)} %all-gather.6.cloned.1.call-done), channel_id=1, source_target_pairs={{0,2},{2,4},{4,6},{6,8},{8,10},{10,12},{12,14},{1,3},{3,5},{5,7},{... | collective-permute-start | bytes 3145736 | tf_op jit(solution)/shard_map/ppermute | solution.py:13
  23.3 149.4 %collective-permute-start.1 = (bf16[512,1024]{1,0:T(8,128)(2,1)}, bf16[512,1024]{1,0:T(8,128)(2,1)S(1)}, u32[]{:S(2)}, u32[]{:S(2)}) collective-permute-start(bf16[512,1024]{1,0:T(8,128)(2,1)} %all-gather.6.cloned.1.call-done), channel_id=1, source_target_pairs={{0,4},{2,6},{4,8},{6,10},{8,12},{10,14},{1,5},{3,7},{5,9},{7,11},{... | collective-permute-start | bytes 3145736 | tf_op jit(solution)/shard_map/ppermute | solution.py:13
  25.3 229.9 %reduce-scatter.3.cloned.1.call-start = ((), (), s32[]{:S(2)}) async-start(), calls=%async_computation.6 | async-start | bytes 1572864 | tf_op jit(solution)/shard_map/reduce_scatter | solution.py:69
  111.2 61.4 %copy-start.2 = (bf16[512,1024]{1,0:T(8,128)(2,1)S(1)}, bf16[512,1024]{1,0:T(8,128)(2,1)}, u32[]{:S(2)}) copy-start(bf16[512,1024]{1,0:T(8,128)(2,1)} %all-gather.6.cloned.1.call-done) | copy-start | bytes 3145732
  180.3 39.6 %copy-start.4 = (f32[512,1024]{1,0:T(8,128)S(1)}, f32[512,1024]{1,0:T(8,128)}, u32[]{:S(2)}) copy-start(f32[512,1024]{1,0:T(8,128)} %fusion.9) | copy-start | bytes 6291460
  209.1 10.8 %copy-start.3 = (bf16[512,1024]{1,0:T(8,128)(2,1)S(1)}, bf16[512,1024]{1,0:T(8,128)(2,1)}, u32[]{:S(2)}) copy-start(bf16[512,1024]{1,0:T(8,128)(2,1)} %all-gather.12.cloned.1.call-done) | copy-start | bytes 3145732
  213.0 70.6 %reduce-scatter.5.cloned.1.call-start = ((), (), s32[]{:S(2)}) async-start(), calls=%async_computation.8 | async-start | bytes 1572864 | tf_op jit(solution)/shard_map/reduce_scatter | solution.py:96
  222.2 29.2 %slice-start = ((s8[6291456]{0:T(1024)(128)(4,1)}), s8[4194304]{0:T(1024)(128)(4,1)S(1)}, s32[]{:S(2)}) async-start(s8[6291456]{0:T(1024)(128)(4,1)} %bitcast.19), calls=%async_computation.9 | async-start | bytes 8388608
  222.4 29.1 %slice-start.1 = ((s8[6291456]{0:T(1024)(128)(4,1)}), s8[2097152]{0:T(1024)(128)(4,1)S(1)}, s32[]{:S(2)}) async-start(s8[6291456]{0:T(1024)(128)(4,1)} %bitcast.19), calls=%async_computation.10 | async-start | bytes 4194304
  222.4 29.0 %collective-permute-start.2 = (bf16[512,1024]{1,0:T(8,128)(2,1)S(1)}, bf16[512,1024]{1,0:T(8,128)(2,1)S(1)}, u32[]{:S(2)}, u32[]{:S(2)}) collective-permute-start(bf16[512,1024]{1,0:T(8,128)(2,1)S(1)} %pad_maximum_fusion), channel_id=1, source_target_pairs={{2,0},{4,2},{6,4},{8,6},{10,8},{12,10},{14,12},{3,1},{5,3},{7,5},{... | collective-permute-start | bytes 3145736 | tf_op jit(solution)/shard_map/ppermute | solution.py:13
  225.1 27.7 %collective-permute-start.3 = (bf16[512,1024]{1,0:T(8,128)(2,1)S(1)}, bf16[512,1024]{1,0:T(8,128)(2,1)S(1)}, u32[]{:S(2)}, u32[]{:S(2)}) collective-permute-start(bf16[512,1024]{1,0:T(8,128)(2,1)S(1)} %pad_maximum_fusion), channel_id=1, source_target_pairs={{4,0},{6,2},{8,4},{10,6},{12,8},{14,10},{5,1},{7,3},{9,5},{11,7},{... | collective-permute-start | bytes 3145736 | tf_op jit(solution)/shard_map/ppermute | solution.py:13
  252.8 2.4 copy-start
  252.8 30.9 %copy-start.1 = (bf16[512,512]{1,0:T(8,128)(2,1)S(1)}, bf16[512,512]{1,0:T(8,128)(2,1)}, u32[]{:S(2)}) copy-start(bf16[512,512]{1,0:T(8,128)(2,1)} %param.13) | copy-start | bytes 1572868
Sparse Core Ops, SparseCore 0:
  9.5 10.3 all-gather.5
  22.1 85.2 all-gather.7
  109.6 59.1 all-gather.9
  170.7 38.3 all-gather.11
  210.5 9.3 all-gather.13
  222.0 9.6 reduce-scatter.2
  255.2 28.3 reduce-scatter.4
where the time goes:
time: 294 us; the launch traced here: 292 us
  waiting for transfers between devices  235 us (80%)
  matrix products  20.3 us (7%)
  between operations  14.3 us (5%)
  starting transfers between devices  10.7 us (4%)
  local copies, waits for them, and re-layouts  7.71 us (3%)
  other arithmetic  4.78 us (2%)
    all_gather x1, waiting for transfers between devices, per_device(): lax.all_gather(filter_weight, 'tm', axis=1, tiled=True)  81.4 us
    all_gather x1, waiting for transfers between devices, per_device(): lax.all_gather(gate_weight, 'tm', axis=1, tiled=True)  57.6 us
    all_gather x1, waiting for transfers between devices, per_device(): lax.all_gather(mix_weight, 'tm', axis=1, tiled=True)  28.8 us
    reduce_scatter x1, waiting for transfers between devices, per_device(): lax.psum_scatter(total.astype(jnp.bfloat16), 'chan', scatter_dimension=1,...  26.5 us
    ppermute x4, waiting for transfers between devices, shifted(): lax.ppermute(value, axis, [(source, source + steps) for source in range(l...  21 us
    ppermute x4, starting transfers between devices, shifted(): lax.ppermute(value, axis, [(source, source + steps) for source in range(l...  10.5 us
    all_gather x1, waiting for transfers between devices, per_device(): whole = lax.all_gather(signal, 'chan', axis=1, tiled=True)  9.91 us
    dot_general x1, matrix products, per_device(): jnp.dot(lagged, stacked.reshape(-1, stacked.shape[2]), preferred_element_...  7.65 us
  transfers between devices with their start and end apart: 11, of which 7 were waited for; matrix products, arithmetic and copies ran while one was open for 11% of the time, Pallas kernels for 0%

commit v1 on v0

--- a/solution.py
+++ b/solution.py
@@ -1,6 +1,8 @@
 import jax
 import jax.numpy as jnp
 from jax import lax
+from jax.experimental import pallas as pl
+from jax.experimental.pallas import tpu as pltpu
 from jax.sharding import PartitionSpec as P
 
 KERNEL_TAPS = 3
@@ -99,6 +101,356 @@
     input_grad = (cotangent.astype(jnp.float32) + input_part).astype(jnp.bfloat16)
     return (output, input_grad)
 
+F32 = jnp.float32
+BF16 = jnp.bfloat16
+NT = (((1,), (1,)), ((), ()))
+DEPTH = 4
+TILE = 256
+
+
+def fused_kernel(
+    signal_ref, filter_ref, gate_ref, fbias_ref, gbias_ref, mixw_ref, cot_ref,
+    out_ref, ig_ref,
+    w, mix, sig, cot, grads, hidden, keep, xout, xin, qout, rin,
+    wsend, wrecv, msend, mrecv, ssend, srecv, fsend, frecv, csend, crecv,
+    xsend, xrecv, qsend, qrecv, local,
+):
+    grp, tm, chan = lax.axis_index("grp"), lax.axis_index("tm"), lax.axis_index("chan")
+    z, x = tm // 2, tm % 2
+    rows = filter_ref.shape[1]
+    half = cot_ref.shape[1]
+    last = 2 * DEPTH - 1
+    circ = (grp + chan) % 2
+    other = 1 - circ
+    here = chan * half
+    there = (1 - chan) * half
+
+    up, down = (grp, tm + 2, chan), (grp, tm - 2, chan)
+    side, twin, mate = (grp, tm + 1 - 2 * x, chan), (1 - grp, tm, chan), (grp, tm, 1 - chan)
+    has_up, has_down = z < DEPTH - 1, z > 0
+    corner_at = tm - 1 + 2 * x
+    has_corner = jnp.logical_and(corner_at >= 0, corner_at <= last)
+
+    def lanes(start, size):
+        return pl.ds(pl.multiple_of(start, 128), size)
+
+    def remote(src, dst, send, recv, to):
+        return pltpu.make_async_remote_copy(
+            src_ref=src, dst_ref=dst, send_sem=send, recv_sem=recv,
+            device_id=to, device_id_type=pl.DeviceIdType.MESH,
+        )
+
+    own_copies = [
+        pltpu.make_async_copy(filter_ref, w.at[0, :, lanes(tm * rows, rows), :], local.at[0]),
+        pltpu.make_async_copy(gate_ref, w.at[1, :, lanes(tm * rows, rows), :], local.at[1]),
+        pltpu.make_async_copy(mixw_ref, mix.at[:, lanes(tm * rows, rows)], local.at[2]),
+        pltpu.make_async_copy(signal_ref, sig.at[0, :, lanes(here, half)], local.at[3]),
+        pltpu.make_async_copy(cot_ref, cot.at[:, lanes(here, half)], local.at[4]),
+    ]
+    for copy in own_copies:
+        copy.start()
+
+    barrier = pltpu.get_barrier_semaphore()
+
+    def greet(to):
+        pl.semaphore_signal(barrier, inc=1, device_id=to, device_id_type=pl.DeviceIdType.MESH)
+
+    greet(side)
+    greet(twin)
+    greet(mate)
+    pl.when(has_up)(lambda: greet(up))
+    pl.when(has_down)(lambda: greet(down))
+    pl.when(has_corner)(lambda: greet((grp, corner_at, chan)))
+    pl.semaphore_wait(
+        barrier,
+        3 + has_up.astype(jnp.int32) + has_down.astype(jnp.int32) + has_corner.astype(jnp.int32),
+    )
+
+    def halo(lag):
+        return remote(
+            sig.at[0, :, lanes(here, half)], sig.at[lag, :, lanes(here, half)],
+            ssend.at[lag], srecv.at[lag], (grp, tm + lag, chan),
+        )
+
+    def to_mate(lag, columns):
+        return remote(
+            sig.at[lag, :, lanes(columns, half)], sig.at[lag, :, lanes(columns, half)],
+            fsend.at[lag], frecv.at[lag], mate,
+        )
+
+    def cot_copy(columns):
+        return remote(
+            cot.at[:, lanes(columns, half)], cot.at[:, lanes(columns, half)],
+            csend.at[0], crecv.at[0], mate,
+        )
+
+    peers = (up, down, side, twin)
+
+    def piece(array, tap, shard, way):
+        slot = w.at[array, tap, lanes(shard * rows, rows), :]
+        return remote(slot, slot, wsend.at[way, tap, shard], wrecv.at[array, tap, shard], peers[way])
+
+    def mix_piece(shard, way):
+        slot = mix.at[:, lanes(shard * rows, rows)]
+        return remote(slot, slot, msend.at[way, shard], mrecv.at[shard], peers[way])
+
+    def each_tap(body):
+        lax.fori_loop(0, KERNEL_TAPS, lambda tap, c: (body(tap), c)[1], 0)
+
+    def ring_round(step, make, act, arrive, hand_over):
+        if step == 0:
+            pl.when(has_up)(lambda: act(make(tm, 0)))
+            pl.when(has_down)(lambda: act(make(tm, 1)))
+            act(make(tm, 2))
+            return
+
+        @pl.when(z >= step)
+        def _():
+            shard = tm - 2 * step
+            arrive(make(shard, 2))
+            pl.when(has_up)(lambda: act(make(shard, 0)))
+            act(make(shard, 2))
+            if hand_over:
+                act(make(shard, 3))
+
+        @pl.when(z + step < DEPTH)
+        def _():
+            shard = tm + 2 * step
+            arrive(make(shard, 2))
+            pl.when(has_down)(lambda: act(make(shard, 1)))
+            act(make(shard, 2))
+            if hand_over:
+                act(make(shard, 3))
+
+    def side_round(step, make, act, arrive, hand_over):
+        def one(shard):
+            arrive(make(shard, 2))
+            if hand_over:
+                act(make(shard, 3))
+
+        base = tm + 1 - 2 * x
+        if step == 0:
+            one(base)
+            return
+        pl.when(z >= step)(lambda: one(base - 2 * step))
+        pl.when(z + step < DEPTH)(lambda: one(base + 2 * step))
+
+    start = lambda copy: copy.start()
+    sent = lambda copy: copy.wait_send()
+    landed = lambda copy: copy.wait_recv()
+    skip = lambda copy: None
+
+    def w_make(tap):
+        return lambda shard, way: piece(circ, tap, shard, way)
+
+    own_copies[3].wait()
+    for lag in (1, 2):
+        pl.when(tm + lag <= last)(lambda: halo(lag).start())
+    own_copies[2].wait()
+    ring_round(0, mix_piece, start, landed, False)
+    own_copies[0].wait()
+    own_copies[1].wait()
+    each_tap(lambda tap: ring_round(0, w_make(tap), start, landed, True))
+    to_mate(0, here).start()
+    own_copies[4].wait()
+    cot_copy(here).start()
+
+    for lag in (1, 2):
+        @pl.when(tm < lag)
+        def _():
+            sig[lag] = jnp.zeros_like(sig[lag])
+
+        @pl.when(tm + lag > last)
+        def _():
+            rin[lag - 1] = jnp.zeros_like(rin[lag - 1])
+
+    for step in range(1, DEPTH):
+        ring_round(step, mix_piece, start, landed, False)
+        side_round(step - 1, mix_piece, start, landed, False)
+
+        def body(tap):
+            ring_round(step, w_make(tap), start, landed, True)
+            side_round(step - 1, w_make(tap), start, landed, True)
+
+        each_tap(body)
+        if step < 3:
+            @pl.when(tm >= step)
+            def _():
+                halo(step).wait_recv()
+                to_mate(step, here).start()
+    side_round(DEPTH - 1, mix_piece, start, landed, False)
+    each_tap(lambda tap: side_round(DEPTH - 1, w_make(tap), start, landed, True))
+
+    to_mate(0, there).wait_recv()
+    for lag in (1, 2):
+        pl.when(tm >= lag)(lambda: to_mate(lag, there).wait_recv())
+    cot_copy(there).wait_recv()
+
+    def other_landed(tap):
+        def one(step, c):
+            piece(other, tap, (tm + step) % (last + 1), 3).wait_recv()
+            return c
+
+        lax.fori_loop(1, last + 1, one, 0)
+
+    each_tap(other_landed)
+
+    def tiles(body):
+        def one(i, c):
+            body(pl.multiple_of(i * TILE, TILE))
+            return c
+
+        lax.fori_loop(0, half // TILE, one, 0)
+
+    def forward(col):
+        columns = pl.ds(col, TILE)
+        pre_f = jnp.broadcast_to(fbias_ref[:, columns], (sig.shape[1], TILE))
+        pre_g = jnp.broadcast_to(gbias_ref[:, columns], (sig.shape[1], TILE))
+        for tap in range(KERNEL_TAPS):
+            pre_f += jnp.dot(sig[tap], w[0, tap, :, columns], preferred_element_type=F32)
+            pre_g += jnp.dot(sig[tap], w[1, tap, :, columns], preferred_element_type=F32)
+        t = jnp.tanh(pre_f)
+        s = jax.nn.sigmoid(pre_g)
+        ts = t * s
+        hidden[:, columns] = ts.astype(BF16)
+        back = lax.dot_general(cot[...], mix[columns, :], NT, preferred_element_type=F32)
+        grads[:, columns] = (back * s * (1.0 - t * t)).astype(BF16)
+        grads[:, pl.ds(pl.multiple_of(half + col, TILE), TILE)] = (back * ts * (1.0 - s)).astype(BF16)
+
+    tiles(forward)
+
+    def grad_part(tap, base, col):
+        channels = pl.ds(pl.multiple_of(base + col, TILE), TILE)
+        return lax.dot_general(
+            grads[:, :half], w[0, tap, channels, :], NT, preferred_element_type=F32
+        ) + lax.dot_general(grads[:, half:], w[1, tap, channels, :], NT, preferred_element_type=F32)
+
+    def mix_part(base, col):
+        channels = pl.ds(pl.multiple_of(base + col, TILE), TILE)
+        return jnp.dot(hidden[...], mix[:, channels], preferred_element_type=F32)
+
+    def swap(slot):
+        return remote(xout.at[slot], xin.at[slot], xsend.at[slot], xrecv.at[slot], mate)
+
+    def back_copy(tap):
+        return remote(
+            qout.at[tap - 1], rin.at[tap - 1], qsend.at[tap - 1], qrecv.at[tap - 1], (grp, tm - tap, chan)
+        )
+
+    def give(slot, part):
+        def one(col):
+            xout[slot, :, pl.ds(col, TILE)] = part(there, col).astype(BF16)
+
+        tiles(one)
+        swap(slot).start()
+
+    def tap_part(tap):
+        return lambda base, col: grad_part(tap, base, col)
+
+    for tap in (2, 1):
+        give(tap, tap_part(tap))
+    for tap in (2, 1):
+        def one(col):
+            keep[:, pl.ds(col, TILE)] = grad_part(tap, here, col)
+
+        tiles(one)
+        swap(tap).wait_recv()
+        qout[tap - 1] = (keep[...] + xin[tap].astype(F32)).astype(BF16)
+        pl.when(tm >= tap)(lambda: back_copy(tap).start())
+    give(3, mix_part)
+    give(0, tap_part(0))
+
+    def out_tile(col):
+        keep[:, pl.ds(col, TILE)] = mix_part(here, col)
+
+    tiles(out_tile)
+    swap(3).wait_recv()
+    out_ref[...] = (
+        sig[0, :, lanes(here, half)].astype(F32) + (keep[...] + xin[3].astype(F32))
+    ).astype(BF16)
+
+    def ig_tile(col):
+        keep[:, pl.ds(col, TILE)] = grad_part(0, here, col)
+
+    tiles(ig_tile)
+    swap(0).wait_recv()
+    keep[...] = keep[...] + xin[0].astype(F32) + cot[:, lanes(here, half)].astype(F32)
+    for tap in (1, 2):
+        pl.when(tm + tap <= last)(lambda: back_copy(tap).wait_recv())
+    ig_ref[...] = (keep[...] + rin[0].astype(F32) + rin[1].astype(F32)).astype(BF16)
+
+    for lag in (1, 2):
+        pl.when(tm + lag <= last)(lambda: halo(lag).wait_send())
+        pl.when(tm >= lag)(lambda: to_mate(lag, here).wait_send())
+        pl.when(tm >= lag)(lambda: back_copy(lag).wait_send())
+    to_mate(0, here).wait_send()
+    cot_copy(here).wait_send()
+    for slot in range(4):
+        swap(slot).wait_send()
+
+    for step in range(DEPTH):
+        ring_round(step, mix_piece, sent, skip, False)
+
+    def drain(tap):
+        for step in range(DEPTH):
+            ring_round(step, w_make(tap), sent, skip, True)
+            side_round(step, w_make(tap), sent, skip, True)
+
+    each_tap(drain)
+
+
+def fused_device(signal, filter_weight, gate_weight, filter_bias, gate_bias, mix_weight, cotangent):
+    steps, half = signal.shape
+    hid = filter_weight.shape[2]
+    count = lax.axis_size("tm")
+    width = count * filter_weight.shape[1]
+    anywhere = pl.BlockSpec(memory_space=pl.ANY)
+    vmem = pl.BlockSpec(memory_space=pltpu.VMEM)
+    dma = pltpu.SemaphoreType.DMA
+    return pl.pallas_call(
+        fused_kernel,
+        out_shape=(
+            jax.ShapeDtypeStruct((steps, half), BF16),
+            jax.ShapeDtypeStruct((steps, half), BF16),
+        ),
+        in_specs=[anywhere, anywhere, anywhere, vmem, vmem, anywhere, anywhere],
+        out_specs=(vmem, vmem),
+        scratch_shapes=[
+            pltpu.VMEM((2, KERNEL_TAPS, width, hid), BF16),
+            pltpu.VMEM((hid, width), BF16),
+            pltpu.VMEM((KERNEL_TAPS, steps, width), BF16),
+            pltpu.VMEM((steps, width), BF16),
+            pltpu.VMEM((steps, 2 * hid), BF16),
+            pltpu.VMEM((steps, hid), BF16),
+            pltpu.VMEM((steps, half), F32),
+            pltpu.VMEM((4, steps, half), BF16),
+            pltpu.VMEM((4, steps, half), BF16),
+            pltpu.VMEM((2, steps, half), BF16),
+            pltpu.VMEM((2, steps, half), BF16),
+            dma((4, KERNEL_TAPS, count)),
+            dma((2, KERNEL_TAPS, count)),
+            dma((3, count)),
+            dma((count,)),
+            dma((3,)),
+            dma((3,)),
+            dma((3,)),
+            dma((3,)),
+            dma((1,)),
+            dma((1,)),
+            dma((4,)),
+            dma((4,)),
+            dma((2,)),
+            dma((2,)),
+            dma((5,)),
+        ],
+        compiler_params=pltpu.CompilerParams(
+            collective_id=0, has_side_effects=True, vmem_limit_bytes=56 * 1024 * 1024
+        ),
+    )(
+        signal, filter_weight, gate_weight, filter_bias.reshape(1, -1), gate_bias.reshape(1, -1),
+        mix_weight, cotangent,
+    )
+
 
 def solution(mesh):
     in_specs = (
@@ -111,6 +463,7 @@
         P(("grp", "tm"), "chan"),
     )
     out_specs = (P(("grp", "tm"), "chan"), P(("grp", "tm"), "chan"))
+    fits = mesh.shape["tm"] == 2 * DEPTH and mesh.shape["grp"] == 2 and mesh.shape["chan"] == 2
     return jax.shard_map(
-        per_device, mesh=mesh, in_specs=in_specs, out_specs=out_specs, check_vma=False
-    )
+        fused_device if fits else per_device, mesh=mesh, in_specs=in_specs, out_specs=out_specs, check_vma=False
+    )

time: 294 us -> 120 us (0.41)
  waiting for transfers between devices: 235 us -> 0 us
  Pallas kernels: 0 us -> 116 us
  matrix products: 20.3 us -> 0 us
  between operations: 14.3 us -> 0.65 us
  starting transfers between devices: 10.7 us -> 0 us
  local copies, waits for them, and re-layouts: 7.71 us -> 2.72 us
  other arithmetic: 4.78 us -> 0 us
    all_gather x5 -> x0, waiting for transfers between devices: 185 us -> none  [the longest x1 81.4 us: per_device(): lax.all_gather(filter_weight, 'tm', axis=1, tiled=True)]
    pallas_call x0 -> x1, Pallas kernels: none -> 116 us  [fused_device(): pl.pallas_call(fused_kernel, out_shape=(jax.ShapeDtypeStruct((steps, half...]
    reduce_scatter x2 -> x0, waiting for transfers between devices: 26.5 us -> none  [the longest x1 26.5 us: per_device(): lax.psum_scatter(total.astype(jnp.bfloat16), 'chan', scatter_dimension=1,...]
    ppermute x4 -> x0, waiting for transfers between devices: 21 us -> none  [shifted(): lax.ppermute(value, axis, [(source, source + steps) for source in range(l...]
    dot_general x6 -> x0, matrix products: 20.3 us -> none  [the longest x1 7.65 us: per_device(): jnp.dot(lagged, stacked.reshape(-1, stacked.shape[2]), preferred_element_...]
    ppermute x4 -> x0, starting transfers between devices: 10.5 us -> none  [shifted(): lax.ppermute(value, axis, [(source, source + steps) for source in range(l...]
    convert_element_type x2 -> x0, other arithmetic: 3.94 us -> none  [the longest x1 1.97 us: per_device(): output = (signal.astype(jnp.float32) + mixed).astype(jnp.bfloat16)]
    concatenate x1 -> x0, local copies, waits for them, and re-layouts: 3.83 us -> none  [per_device(): stacked = jnp.concatenate([filter_full, gate_full], axis=2)]
  transfers between devices with their start and end apart: 11 -> 0, of which waited for: 7 -> 0; matrix products, arithmetic and copies ran while one was open for 11% -> 0% of each run, Pallas kernels for 0% -> 0%
where the time goes in v1:
time: 120 us
  Pallas kernels  116 us (97%)
  local copies, waits for them, and re-layouts  2.72 us (2%)
    pallas_call x1, Pallas kernels, fused_device(): pl.pallas_call(fused_kernel, out_shape=(jax.ShapeDtypeStruct((steps, half...  116 us
    unnamed x4, local copies, waits for them, and re-layouts  2.72 us

profile of v1, /device:TPU:18, one launch (start us, length us, event | category | flops | bytes accessed | tf_op | source)
XLA Modules:
  0.0 119.8 jit_solution(18030468256557143122)
XLA Ops:
  0.6 116.4 %shard_map.86 = (bf16[512,512]{1,0:T(8,128)(2,1)}, bf16[512,512]{1,0:T(8,128)(2,1)}) custom-call(bf16[512,512]{1,0:T(8,128)(2,1)} %signal_ref.1, bf16[3,128,512]{2,1,0:T(8,128)(2,1)} %filter_ref.1, bf16[3,128,512]{2,1,0:T(8,128)(2,1)} %gate_ref.1, f32[1,512]{1,0:T(1,128)} %bitcast.2, f32[1,512]{1,0:T(1,128)} %bitcast.3, bf16[512,128]{1,0:T(8,128)(2,1)} %mixw_ref.1, ...), custom_call_target="tpu_custom_call" | custom-call | tf_op jit(solution)/shard_map/pallas_call | solution.py:410
  117.0 0.0 copy-start
  117.0 1.9 %copy.11 = bf16[512,512]{1,0:T(8,128)(2,1)} copy(bf16[512,512]{1,0:T(8,128)(2,1)} %get-tuple-element.4) | data formatting | bytes 1048576
  119.0 0.0 copy-done
  119.0 0.8 copy.12
Async XLA Ops:
  117.0 1.9 %copy-start = (bf16[512,512]{1,0:T(8,128)(2,1)S(1)}, bf16[512,512]{1,0:T(8,128)(2,1)}, u32[]{:S(2)}) copy-start(bf16[512,512]{1,0:T(8,128)(2,1)} %get-tuple-element.5) | copy-start | bytes 1572868

commit v2 on v1

--- a/solution.py
+++ b/solution.py
@@ -166,10 +166,10 @@
         3 + has_up.astype(jnp.int32) + has_down.astype(jnp.int32) + has_corner.astype(jnp.int32),
     )
 
-    def halo(lag):
+    def halo(held, lag, to):
         return remote(
-            sig.at[0, :, lanes(here, half)], sig.at[lag, :, lanes(here, half)],
-            ssend.at[lag], srecv.at[lag], (grp, tm + lag, chan),
+            sig.at[held, :, lanes(here, half)], sig.at[lag, :, lanes(here, half)],
+            ssend.at[lag], srecv.at[lag], to,
         )
 
     def to_mate(lag, columns):
@@ -244,13 +244,13 @@
         return lambda shard, way: piece(circ, tap, shard, way)
 
     own_copies[3].wait()
-    for lag in (1, 2):
-        pl.when(tm + lag <= last)(lambda: halo(lag).start())
     own_copies[2].wait()
     ring_round(0, mix_piece, start, landed, False)
     own_copies[0].wait()
     own_copies[1].wait()
     each_tap(lambda tap: ring_round(0, w_make(tap), start, landed, True))
+    pl.when(has_up)(lambda: halo(0, 2, up).start())
+    pl.when(x == 0)(lambda: halo(0, 1, side).start())
     to_mate(0, here).start()
     own_copies[4].wait()
     cot_copy(here).start()
@@ -273,11 +273,18 @@
             side_round(step - 1, w_make(tap), start, landed, True)
 
         each_tap(body)
-        if step < 3:
-            @pl.when(tm >= step)
+        if step == 1:
+            @pl.when(has_down)
             def _():
-                halo(step).wait_recv()
-                to_mate(step, here).start()
+                halo(0, 2, side).wait_recv()
+                pl.when(x == 1)(lambda: halo(2, 1, side).start())
+                to_mate(2, here).start()
+
+        if step == 2:
+            @pl.when(tm >= 1)
+            def _():
+                halo(0, 1, side).wait_recv()
+                to_mate(1, here).start()
     side_round(DEPTH - 1, mix_piece, start, landed, False)
     each_tap(lambda tap: side_round(DEPTH - 1, w_make(tap), start, landed, True))
 
@@ -379,8 +386,10 @@
         pl.when(tm + tap <= last)(lambda: back_copy(tap).wait_recv())
     ig_ref[...] = (keep[...] + rin[0].astype(F32) + rin[1].astype(F32)).astype(BF16)
 
+    pl.when(has_up)(lambda: halo(0, 2, up).wait_send())
+    pl.when(x == 0)(lambda: halo(0, 1, side).wait_send())
+    pl.when(jnp.logical_and(x == 1, has_down))(lambda: halo(2, 1, side).wait_send())
     for lag in (1, 2):
-        pl.when(tm + lag <= last)(lambda: halo(lag).wait_send())
         pl.when(tm >= lag)(lambda: to_mate(lag, here).wait_send())
         pl.when(tm >= lag)(lambda: back_copy(lag).wait_send())
     to_mate(0, here).wait_send()

time: 120 us -> 114 us (0.950)
  Pallas kernels: 116 us -> 110 us
    pallas_call x1, Pallas kernels: 116 us -> 110 us  [fused_device(): pl.pallas_call(fused_kernel, out_shape=(jax.ShapeDtypeStruct((steps, half...]
where the time goes in v2:
time: 114 us
  Pallas kernels  110 us (96%)
  local copies, waits for them, and re-layouts  2.72 us (2%)
    pallas_call x1, Pallas kernels, fused_device(): pl.pallas_call(fused_kernel, out_shape=(jax.ShapeDtypeStruct((steps, half...  110 us
    unnamed x4, local copies, waits for them, and re-layouts  2.72 us

profile of v2, /device:TPU:18, one launch (start us, length us, event | category | flops | bytes accessed | tf_op | source)
XLA Modules:
  0.0 113.6 jit_solution(7530913689659499674)
XLA Ops:
  0.6 110.2 %shard_map.86 = (bf16[512,512]{1,0:T(8,128)(2,1)}, bf16[512,512]{1,0:T(8,128)(2,1)}) custom-call(bf16[512,512]{1,0:T(8,128)(2,1)} %signal_ref.1, bf16[3,128,512]{2,1,0:T(8,128)(2,1)} %filter_ref.1, bf16[3,128,512]{2,1,0:T(8,128)(2,1)} %gate_ref.1, f32[1,512]{1,0:T(1,128)} %bitcast.2, f32[1,512]{1,0:T(1,128)} %bitcast.3, bf16[512,128]{1,0:T(8,128)(2,1)} %mixw_ref.1, ...), custom_call_target="tpu_custom_call" | custom-call | tf_op jit(solution)/shard_map/pallas_call | solution.py:419
  110.8 0.0 copy-start
  110.8 1.9 %copy.11 = bf16[512,512]{1,0:T(8,128)(2,1)} copy(bf16[512,512]{1,0:T(8,128)(2,1)} %get-tuple-element.4) | data formatting | bytes 1048576
  112.8 0.0 copy-done
  112.8 0.8 copy.12
Async XLA Ops:
  110.8 1.9 %copy-start = (bf16[512,512]{1,0:T(8,128)(2,1)S(1)}, bf16[512,512]{1,0:T(8,128)(2,1)}, u32[]{:S(2)}) copy-start(bf16[512,512]{1,0:T(8,128)(2,1)} %get-tuple-element.5) | copy-start | bytes 1572868

commit v3 on v2

--- a/solution.py
+++ b/solution.py
@@ -113,7 +113,7 @@
     out_ref, ig_ref,
     w, mix, sig, cot, grads, hidden, keep, xout, xin, qout, rin,
     wsend, wrecv, msend, mrecv, ssend, srecv, fsend, frecv, csend, crecv,
-    xsend, xrecv, qsend, qrecv, local,
+    xsend, xrecv, qsend, qrecv, local, pre, backs,
 ):
     grp, tm, chan = lax.axis_index("grp"), lax.axis_index("tm"), lax.axis_index("chan")
     z, x = tm // 2, tm % 2
@@ -300,8 +300,6 @@
 
         lax.fori_loop(1, last + 1, one, 0)
 
-    each_tap(other_landed)
-
     def tiles(body):
         def one(i, c):
             body(pl.multiple_of(i * TILE, TILE))
@@ -309,18 +307,35 @@
 
         lax.fori_loop(0, half // TILE, one, 0)
 
+    def early(col):
+        columns = pl.ds(col, TILE)
+        total = jnp.dot(sig[0], w[circ, 0, :, columns], preferred_element_type=F32)
+        for tap in range(1, KERNEL_TAPS):
+            total += jnp.dot(sig[tap], w[circ, tap, :, columns], preferred_element_type=F32)
+        pre[circ, :, columns] = total
+        backs[:, columns] = lax.dot_general(cot[...], mix[columns, :], NT, preferred_element_type=F32)
+
+    tiles(early)
+
+    for tap in range(KERNEL_TAPS):
+        other_landed(tap)
+
+        def late(col):
+            columns = pl.ds(col, TILE)
+            part = jnp.dot(sig[tap], w[other, tap, :, columns], preferred_element_type=F32)
+            pre[other, :, columns] = part if tap == 0 else pre[other, :, columns] + part
+
+        tiles(late)
+
     def forward(col):
         columns = pl.ds(col, TILE)
-        pre_f = jnp.broadcast_to(fbias_ref[:, columns], (sig.shape[1], TILE))
-        pre_g = jnp.broadcast_to(gbias_ref[:, columns], (sig.shape[1], TILE))
-        for tap in range(KERNEL_TAPS):
-            pre_f += jnp.dot(sig[tap], w[0, tap, :, columns], preferred_element_type=F32)
-            pre_g += jnp.dot(sig[tap], w[1, tap, :, columns], preferred_element_type=F32)
+        pre_f = pre[0, :, columns] + fbias_ref[:, columns]
+        pre_g = pre[1, :, columns] + gbias_ref[:, columns]
         t = jnp.tanh(pre_f)
         s = jax.nn.sigmoid(pre_g)
         ts = t * s
         hidden[:, columns] = ts.astype(BF16)
-        back = lax.dot_general(cot[...], mix[columns, :], NT, preferred_element_type=F32)
+        back = backs[:, columns]
         grads[:, columns] = (back * s * (1.0 - t * t)).astype(BF16)
         grads[:, pl.ds(pl.multiple_of(half + col, TILE), TILE)] = (back * ts * (1.0 - s)).astype(BF16)
 
@@ -451,6 +466,8 @@
             dma((2,)),
             dma((2,)),
             dma((5,)),
+            pltpu.VMEM((2, steps, hid), F32),
+            pltpu.VMEM((steps, hid), F32),
         ],
         compiler_params=pltpu.CompilerParams(
             collective_id=0, has_side_effects=True, vmem_limit_bytes=56 * 1024 * 1024

time: 114 us -> 111 us (0.974)
  Pallas kernels: 110 us -> 107 us
    pallas_call x1, Pallas kernels: 110 us -> 107 us  [fused_device(): pl.pallas_call(fused_kernel, out_shape=(jax.ShapeDtypeStruct((steps, half...]
where the time goes in v3:
time: 111 us
  Pallas kernels  107 us (96%)
  local copies, waits for them, and re-layouts  2.72 us (2%)
    pallas_call x1, Pallas kernels, fused_device(): pl.pallas_call(fused_kernel, out_shape=(jax.ShapeDtypeStruct((steps, half...  107 us
    unnamed x4, local copies, waits for them, and re-layouts  2.72 us

profile of v3, /device:TPU:18, one launch (start us, length us, event | category | flops | bytes accessed | tf_op | source)
XLA Modules:
  0.0 110.7 jit_solution(4990137038944492149)
XLA Ops:
  0.6 107.3 %shard_map.86 = (bf16[512,512]{1,0:T(8,128)(2,1)}, bf16[512,512]{1,0:T(8,128)(2,1)}) custom-call(bf16[512,512]{1,0:T(8,128)(2,1)} %signal_ref.1, bf16[3,128,512]{2,1,0:T(8,128)(2,1)} %filter_ref.1, bf16[3,128,512]{2,1,0:T(8,128)(2,1)} %gate_ref.1, f32[1,512]{1,0:T(1,128)} %bitcast.2, f32[1,512]{1,0:T(1,128)} %bitcast.3, bf16[512,128]{1,0:T(8,128)(2,1)} %mixw_ref.1, ...), custom_call_target="tpu_custom_call" | custom-call | tf_op jit(solution)/shard_map/pallas_call | solution.py:434
  107.9 0.0 copy-start
  107.9 1.9 %copy.11 = bf16[512,512]{1,0:T(8,128)(2,1)} copy(bf16[512,512]{1,0:T(8,128)(2,1)} %get-tuple-element.4) | data formatting | bytes 1048576
  109.9 0.0 copy-done
  109.9 0.8 copy.12
Async XLA Ops:
  107.9 1.9 %copy-start = (bf16[512,512]{1,0:T(8,128)(2,1)S(1)}, bf16[512,512]{1,0:T(8,128)(2,1)}, u32[]{:S(2)}) copy-start(bf16[512,512]{1,0:T(8,128)(2,1)} %get-tuple-element.5) | copy-start | bytes 1572868

commit v4 on v3

--- a/solution.py
+++ b/solution.py
@@ -106,6 +106,7 @@
 NT = (((1,), (1,)), ((), ()))
 DEPTH = 4
 TILE = 256
+CHUNKS = 4
 
 
 def fused_kernel(
@@ -128,8 +129,6 @@
     up, down = (grp, tm + 2, chan), (grp, tm - 2, chan)
     side, twin, mate = (grp, tm + 1 - 2 * x, chan), (1 - grp, tm, chan), (grp, tm, 1 - chan)
     has_up, has_down = z < DEPTH - 1, z > 0
-    corner_at = tm - 1 + 2 * x
-    has_corner = jnp.logical_and(corner_at >= 0, corner_at <= last)
 
     def lanes(start, size):
         return pl.ds(pl.multiple_of(start, 128), size)
@@ -160,11 +159,7 @@
     greet(mate)
     pl.when(has_up)(lambda: greet(up))
     pl.when(has_down)(lambda: greet(down))
-    pl.when(has_corner)(lambda: greet((grp, corner_at, chan)))
-    pl.semaphore_wait(
-        barrier,
-        3 + has_up.astype(jnp.int32) + has_down.astype(jnp.int32) + has_corner.astype(jnp.int32),
-    )
+    pl.semaphore_wait(barrier, 3 + has_up.astype(jnp.int32) + has_down.astype(jnp.int32))
 
     def halo(held, lag, to):
         return remote(
@@ -260,19 +255,18 @@
         def _():
             sig[lag] = jnp.zeros_like(sig[lag])
 
-        @pl.when(tm + lag > last)
-        def _():
-            rin[lag - 1] = jnp.zeros_like(rin[lag - 1])
+    @pl.when(jnp.logical_not(has_up))
+    def _():
+        rin[1] = jnp.zeros_like(rin[1])
 
     for step in range(1, DEPTH):
-        ring_round(step, mix_piece, start, landed, False)
-        side_round(step - 1, mix_piece, start, landed, False)
-
         def body(tap):
             ring_round(step, w_make(tap), start, landed, True)
             side_round(step - 1, w_make(tap), start, landed, True)
 
         each_tap(body)
+        ring_round(step, mix_piece, start, landed, False)
+        side_round(step - 1, mix_piece, start, landed, False)
         if step == 1:
             @pl.when(has_down)
             def _():
@@ -354,10 +348,21 @@
     def swap(slot):
         return remote(xout.at[slot], xin.at[slot], xsend.at[slot], xrecv.at[slot], mate)
 
-    def back_copy(tap):
+    chunk = rin.shape[1] // CHUNKS
+
+    def back_copy(tap, part):
+        piece_rows = pl.ds(part * chunk, chunk)
         return remote(
-            qout.at[tap - 1], rin.at[tap - 1], qsend.at[tap - 1], qrecv.at[tap - 1], (grp, tm - tap, chan)
+            qout.at[tap - 1, piece_rows], rin.at[tap - 1, piece_rows],
+            qsend.at[tap - 1, part], qrecv.at[tap - 1, part], side if tap == 1 else down,
         )
+
+    def all_parts(tap, act):
+        for part in range(CHUNKS):
+            act(back_copy(tap, part))
+
+    side_gives = jnp.logical_or(x == 1, has_down)
+    merges = jnp.logical_and(x == 1, has_down)
 
     def give(slot, part):
         def one(col):
@@ -369,18 +374,35 @@
     def tap_part(tap):
         return lambda base, col: grad_part(tap, base, col)
 
-    for tap in (2, 1):
+    for tap in (1, 2):
         give(tap, tap_part(tap))
-    for tap in (2, 1):
+    for tap in (1, 2):
         def one(col):
             keep[:, pl.ds(col, TILE)] = grad_part(tap, here, col)
 
         tiles(one)
         swap(tap).wait_recv()
-        qout[tap - 1] = (keep[...] + xin[tap].astype(F32)).astype(BF16)
-        pl.when(tm >= tap)(lambda: back_copy(tap).start())
+        if tap == 1:
+            qout[0] = (keep[...] + xin[1].astype(F32)).astype(BF16)
+            pl.when(side_gives)(lambda: all_parts(1, start))
+
+    keep[...] = keep[...] + xin[2].astype(F32)
+
+    @pl.when(jnp.logical_and(x == 0, has_down))
+    def _():
+        qout[1] = keep[...].astype(BF16)
+        all_parts(2, start)
+
     give(3, mix_part)
     give(0, tap_part(0))
+
+    @pl.when(merges)
+    def _():
+        for part in range(CHUNKS):
+            back_copy(1, part).wait_recv()
+            piece_rows = pl.ds(part * chunk, chunk)
+            qout[1, piece_rows] = (keep[piece_rows] + rin[0, piece_rows].astype(F32)).astype(BF16)
+            back_copy(2, part).start()
 
     def out_tile(col):
         keep[:, pl.ds(col, TILE)] = mix_part(here, col)
@@ -397,20 +419,26 @@
     tiles(ig_tile)
     swap(0).wait_recv()
     keep[...] = keep[...] + xin[0].astype(F32) + cot[:, lanes(here, half)].astype(F32)
-    for tap in (1, 2):
-        pl.when(tm + tap <= last)(lambda: back_copy(tap).wait_recv())
-    ig_ref[...] = (keep[...] + rin[0].astype(F32) + rin[1].astype(F32)).astype(BF16)
+
+    @pl.when(x == 0)
+    def _():
+        all_parts(1, landed)
+        keep[...] = keep[...] + rin[0].astype(F32)
+
+    pl.when(has_up)(lambda: all_parts(2, landed))
+    ig_ref[...] = (keep[...] + rin[1].astype(F32)).astype(BF16)
 
     pl.when(has_up)(lambda: halo(0, 2, up).wait_send())
     pl.when(x == 0)(lambda: halo(0, 1, side).wait_send())
     pl.when(jnp.logical_and(x == 1, has_down))(lambda: halo(2, 1, side).wait_send())
     for lag in (1, 2):
         pl.when(tm >= lag)(lambda: to_mate(lag, here).wait_send())
-        pl.when(tm >= lag)(lambda: back_copy(lag).wait_send())
     to_mate(0, here).wait_send()
     cot_copy(here).wait_send()
     for slot in range(4):
         swap(slot).wait_send()
+    pl.when(side_gives)(lambda: all_parts(1, sent))
+    pl.when(has_down)(lambda: all_parts(2, sent))
 
     for step in range(DEPTH):
         ring_round(step, mix_piece, sent, skip, False)
@@ -463,8 +491,8 @@
             dma((1,)),
             dma((4,)),
             dma((4,)),
-            dma((2,)),
-            dma((2,)),
+            dma((2, CHUNKS)),
+            dma((2, CHUNKS)),
             dma((5,)),
             pltpu.VMEM((2, steps, hid), F32),
             pltpu.VMEM((steps, hid), F32),

time: 111 us -> 101 us (0.910)
  Pallas kernels: 107 us -> 97.4 us
    pallas_call x1, Pallas kernels: 107 us -> 97.4 us  [fused_device(): pl.pallas_call(fused_kernel, out_shape=(jax.ShapeDtypeStruct((steps, half...]
where the time goes in v4:
time: 101 us
  Pallas kernels  97.4 us (96%)
  local copies, waits for them, and re-layouts  2.72 us (3%)
    pallas_call x1, Pallas kernels, fused_device(): pl.pallas_call(fused_kernel, out_shape=(jax.ShapeDtypeStruct((steps, half...  97.4 us
    unnamed x4, local copies, waits for them, and re-layouts  2.72 us

profile of v4, /device:TPU:18, one launch (start us, length us, event | category | flops | bytes accessed | tf_op | source)
XLA Modules:
  0.0 100.8 jit_solution(16564665601566804988)
XLA Ops:
  0.6 97.4 %shard_map.86 = (bf16[512,512]{1,0:T(8,128)(2,1)}, bf16[512,512]{1,0:T(8,128)(2,1)}) custom-call(bf16[512,512]{1,0:T(8,128)(2,1)} %signal_ref.1, bf16[3,128,512]{2,1,0:T(8,128)(2,1)} %filter_ref.1, bf16[3,128,512]{2,1,0:T(8,128)(2,1)} %gate_ref.1, f32[1,512]{1,0:T(1,128)} %bitcast.2, f32[1,512]{1,0:T(1,128)} %bitcast.3, bf16[512,128]{1,0:T(8,128)(2,1)} %mixw_ref.1, ...), custom_call_target="tpu_custom_call" | custom-call | tf_op jit(solution)/shard_map/pallas_call | solution.py:462
  98.1 0.0 copy-start
  98.1 1.9 %copy.11 = bf16[512,512]{1,0:T(8,128)(2,1)} copy(bf16[512,512]{1,0:T(8,128)(2,1)} %get-tuple-element.4) | data formatting | bytes 1048576
  100.0 0.0 copy-done
  100.0 0.8 copy.12
Async XLA Ops:
  98.1 1.9 %copy-start = (bf16[512,512]{1,0:T(8,128)(2,1)S(1)}, bf16[512,512]{1,0:T(8,128)(2,1)}, u32[]{:S(2)}) copy-start(bf16[512,512]{1,0:T(8,128)(2,1)} %get-tuple-element.5) | copy-start | bytes 1572868

commit v5 on v4

--- a/solution.py
+++ b/solution.py
@@ -106,7 +106,7 @@
 NT = (((1,), (1,)), ((), ()))
 DEPTH = 4
 TILE = 256
-CHUNKS = 4
+CHUNKS = 8
 
 
 def fused_kernel(
@@ -114,7 +114,7 @@
     out_ref, ig_ref,
     w, mix, sig, cot, grads, hidden, keep, xout, xin, qout, rin,
     wsend, wrecv, msend, mrecv, ssend, srecv, fsend, frecv, csend, crecv,
-    xsend, xrecv, qsend, qrecv, local, pre, backs,
+    xsend, xrecv, qsend, qrecv, local, pre, backs, mix_parts,
 ):
     grp, tm, chan = lax.axis_index("grp"), lax.axis_index("tm"), lax.axis_index("chan")
     z, x = tm // 2, tm % 2
@@ -142,7 +142,7 @@
     own_copies = [
         pltpu.make_async_copy(filter_ref, w.at[0, :, lanes(tm * rows, rows), :], local.at[0]),
         pltpu.make_async_copy(gate_ref, w.at[1, :, lanes(tm * rows, rows), :], local.at[1]),
-        pltpu.make_async_copy(mixw_ref, mix.at[:, lanes(tm * rows, rows)], local.at[2]),
+        pltpu.make_async_copy(mixw_ref, mix_parts.at[tm], local.at[2]),
         pltpu.make_async_copy(signal_ref, sig.at[0, :, lanes(here, half)], local.at[3]),
         pltpu.make_async_copy(cot_ref, cot.at[:, lanes(here, half)], local.at[4]),
     ]
@@ -186,7 +186,7 @@
         return remote(slot, slot, wsend.at[way, tap, shard], wrecv.at[array, tap, shard], peers[way])
 
     def mix_piece(shard, way):
-        slot = mix.at[:, lanes(shard * rows, rows)]
+        slot = mix_parts.at[shard]
         return remote(slot, slot, msend.at[way, shard], mrecv.at[shard], peers[way])
 
     def each_tap(body):
@@ -240,12 +240,11 @@
 
     own_copies[3].wait()
     own_copies[2].wait()
-    ring_round(0, mix_piece, start, landed, False)
     own_copies[0].wait()
     own_copies[1].wait()
     each_tap(lambda tap: ring_round(0, w_make(tap), start, landed, True))
+    ring_round(0, mix_piece, start, landed, False)
     pl.when(has_up)(lambda: halo(0, 2, up).start())
-    pl.when(x == 0)(lambda: halo(0, 1, side).start())
     to_mate(0, here).start()
     own_copies[4].wait()
     cot_copy(here).start()
@@ -261,13 +260,15 @@
 
     for step in range(1, DEPTH):
         def body(tap):
+            side_round(step - 1, w_make(tap), start, landed, True)
             ring_round(step, w_make(tap), start, landed, True)
-            side_round(step - 1, w_make(tap), start, landed, True)
 
         each_tap(body)
         ring_round(step, mix_piece, start, landed, False)
         side_round(step - 1, mix_piece, start, landed, False)
         if step == 1:
+            pl.when(x == 0)(lambda: halo(0, 1, side).start())
+
             @pl.when(has_down)
             def _():
                 halo(0, 2, side).wait_recv()
@@ -309,6 +310,8 @@
         pre[circ, :, columns] = total
         backs[:, columns] = lax.dot_general(cot[...], mix[columns, :], NT, preferred_element_type=F32)
 
+    for shard in range(last + 1):
+        mix[:, shard * rows : (shard + 1) * rows] = mix_parts[shard]
     tiles(early)
 
     for tap in range(KERNEL_TAPS):
@@ -496,6 +499,7 @@
             dma((5,)),
             pltpu.VMEM((2, steps, hid), F32),
             pltpu.VMEM((steps, hid), F32),
+            pltpu.VMEM((count, hid, width // count), BF16),
         ],
         compiler_params=pltpu.CompilerParams(
             collective_id=0, has_side_effects=True, vmem_limit_bytes=56 * 1024 * 1024

time: 101 us -> 98.6 us (0.976)
  Pallas kernels: 97.4 us -> 95 us
    pallas_call x1, Pallas kernels: 97.4 us -> 95 us  [fused_device(): pl.pallas_call(fused_kernel, out_shape=(jax.ShapeDtypeStruct((steps, half...]
where the time goes in v5:
time: 98.6 us; the launch traced here: 98.4 us
  Pallas kernels  95 us (96%)
  local copies, waits for them, and re-layouts  2.72 us (3%)
    pallas_call x1, Pallas kernels, fused_device(): pl.pallas_call(fused_kernel, out_shape=(jax.ShapeDtypeStruct((steps, half...  95 us
    unnamed x4, local copies, waits for them, and re-layouts  2.72 us

profile of v5, /device:TPU:18, one launch (start us, length us, event | category | flops | bytes accessed | tf_op | source)
XLA Modules:
  0.0 98.4 jit_solution(15570158618043392276)
XLA Ops:
  0.6 95.0 %shard_map.86 = (bf16[512,512]{1,0:T(8,128)(2,1)}, bf16[512,512]{1,0:T(8,128)(2,1)}) custom-call(bf16[512,512]{1,0:T(8,128)(2,1)} %signal_ref.1, bf16[3,128,512]{2,1,0:T(8,128)(2,1)} %filter_ref.1, bf16[3,128,512]{2,1,0:T(8,128)(2,1)} %gate_ref.1, f32[1,512]{1,0:T(1,128)} %bitcast.2, f32[1,512]{1,0:T(1,128)} %bitcast.3, bf16[512,128]{1,0:T(8,128)(2,1)} %mixw_ref.1, ...), custom_call_target="tpu_custom_call" | custom-call | tf_op jit(solution)/shard_map/pallas_call | solution.py:465
  95.7 0.0 copy-start
  95.7 1.9 %copy.11 = bf16[512,512]{1,0:T(8,128)(2,1)} copy(bf16[512,512]{1,0:T(8,128)(2,1)} %get-tuple-element.4) | data formatting | bytes 1048576
  97.6 0.0 copy-done
  97.6 0.8 copy.12
Async XLA Ops:
  95.7 1.9 %copy-start = (bf16[512,512]{1,0:T(8,128)(2,1)S(1)}, bf16[512,512]{1,0:T(8,128)(2,1)}, u32[]{:S(2)}) copy-start(bf16[512,512]{1,0:T(8,128)(2,1)} %get-tuple-element.5) | copy-start | bytes 1572868
